TPU v7x, 32 devices: a whole 2x2x4 slice. The times are simulated.
32 devices in a mesh: seq: 8 (over z, y), fsdp: 4 (over x, core).
Axes of the slice: x: 2, y: 2, z: 4, core: 2. Of those that a mesh axis runs over, the one named last changes fastest.
Arguments:
- tokens: bfloat16 [8192, 4096], P('seq', 'fsdp'), may hold values from -6 to 6
- projection: bfloat16 [3, 4096, 2048], P(None, 'seq', 'fsdp'), may hold values from -0.09375 to 0.09375
- log_decay: float32 [8192, 16], P('seq', 'fsdp'), may hold values from -2 to 0, as said below
Outputs:
- attended: bfloat16 [8192, 2048], P('seq', 'fsdp')
Inputs may be any that keep to these rules, and one draw needn't show every extreme that they name: `log_decay`: negative logarithms of decay factors, one for each position and head.
All inputs are finite; a program needn't handle non-finite values.
Results may differ from a plain program's by a relative error of at most 0.006.
Values may be sent and summed in bfloat16 or wider, within the bound.
A program may use at most 64 MiB of HBM per device.

v0:
```python
import jax
import jax.numpy as jnp
from jax import lax
from jax.sharding import PartitionSpec as P

BLK = 512


def entering(part, axis, combine, identity):
    place = lax.axis_index(axis)
    gathered = jax.tree.map(lambda a: lax.all_gather(a, axis), part)
    state = jax.tree.map(lambda a, e: jnp.zeros_like(a) + jnp.asarray(e, a.dtype), part, identity)

    def one(hop, state):
        return combine(
            state, jax.tree.map(lambda a: lax.dynamic_index_in_dim(a, hop, 0, False), gathered)
        )

    return lax.fori_loop(0, place, one, state)


def local_states(key_vecs, value_vecs, decay):
    running = jnp.cumsum(decay, axis=1)
    last = running[:, -1]
    carried = key_vecs.astype(jnp.float32) * jnp.exp(last[:, None, :] - running)[..., None]
    fresh = jnp.einsum(
        "nshd,nshe->nhde", carried, value_vecs.astype(jnp.float32), precision=lax.Precision.HIGHEST
    )

    def advance(state, inputs):
        block_last, block_fresh = inputs
        return (jnp.exp(block_last)[:, None, None] * state + block_fresh, state)

    start = jnp.zeros(fresh.shape[1:], jnp.float32)
    final, before = lax.scan(advance, start, (last, fresh))
    leading = jnp.cumsum(last, axis=0) - last
    whole_decay = jnp.exp(jnp.sum(last, axis=0))
    return (final, before, leading, whole_decay)


def combine(earlier, later):
    return (earlier[0] * later[0], later[0][:, None, None] * earlier[1] + later[1])


def chain(key_raw, value_raw, decay, shaped):
    key_vecs = shaped(jax.nn.silu(key_raw).astype(jnp.bfloat16))
    value_vecs = shaped(value_raw.astype(jnp.bfloat16))
    final, before, leading, whole_decay = local_states(key_vecs, value_vecs, decay)
    identity = (jnp.ones_like(whole_decay), jnp.zeros_like(final))
    carry = entering((whole_decay, final), "seq", combine, identity)
    incoming = before + jnp.exp(leading)[:, :, None, None] * carry[1][None]
    return (key_vecs, value_vecs, incoming)


def attend_block(inputs):
    queries, key_vecs, value_vecs, decay, state = inputs
    running = jnp.cumsum(decay, axis=0)
    across = running.T
    gap = across[:, :, None] - across[:, None, :]
    lower = jnp.arange(gap.shape[1])[:, None] >= jnp.arange(gap.shape[2])[None, :]
    fading = jnp.exp(jnp.where(lower[None], gap, -1e30))
    scores = jnp.einsum("thd,shd->hts", queries, key_vecs, preferred_element_type=jnp.float32)
    weights = (fading * scores).astype(jnp.bfloat16)
    intra = jnp.einsum("hts,she->the", weights, value_vecs, preferred_element_type=jnp.float32)
    inter = jnp.exp(running)[:, :, None] * jnp.einsum(
        "thd,hde->the", queries.astype(jnp.float32), state, precision=lax.Precision.HIGHEST
    )
    mixed = intra + inter
    normed = mixed * lax.rsqrt(jnp.mean(mixed * mixed, axis=-1, keepdims=True) + 1e-06)
    return normed.astype(jnp.bfloat16)


def on_device(tokens, projection, log_decay):
    features = lax.all_gather(tokens, "fsdp", axis=1, tiled=True)
    rows = features.shape[0]
    heads = log_decay.shape[1]
    width = projection.shape[2]
    head = width // heads
    blocks = rows // BLK

    def shaped(matrix):
        return matrix.reshape(blocks, BLK, heads, head)

    decay = log_decay.reshape(blocks, BLK, heads)
    raw = jnp.einsum(
        "td,cdn->ctn",
        features,
        lax.all_gather(projection, "seq", axis=1, tiled=True),
        preferred_element_type=jnp.float32,
    )
    key_vecs, value_vecs, incoming = chain(raw[1], raw[2], decay, shaped)
    query_raw = raw[0]
    queries = shaped(jax.nn.silu(query_raw).astype(jnp.bfloat16))
    outputs = lax.map(attend_block, (queries, key_vecs, value_vecs, decay, incoming))
    return outputs.reshape(rows, width)


def solution(mesh):
    in_specs = (P("seq", "fsdp"), P(None, "seq", "fsdp"), P("seq", "fsdp"))
    out_specs = P("seq", "fsdp")
    return jax.shard_map(
        on_device, mesh=mesh, in_specs=in_specs, out_specs=out_specs, check_vma=False
    )
```

profile of v0, /device:TPU:24, one launch (start us, length us, event | category | flops | bytes accessed | tf_op | source)
XLA Modules:
  0.0 364.0 jit_solution(7133900200984895879)
XLA Ops:
  7.9 1.6 copy.52
  9.7 2.4 reduce-window.14
  13.0 55.2 %all-gather.8.cloned.1.call-done = bf16[1024,4096]{1,0:T(8,128)(2,1)} async-done(((bf16[1024,1024]{1,0:T(8,128)(2,1)}), bf16[1024,4096]{1,0:T(8,128)(2,1)}) %all-gather.8.cloned.1.call-update) | async-done | bytes 8388624 | tf_op jit(solution)/shard_map/all_gather | solution.py:74
  68.2 176.8 %all-gather.6.cloned.1.call-done = bf16[3,4096,512]{1,2,0:T(8,128)(2,1)} async-done(((bf16[3,512,512]{1,2,0:T(8,128)(2,1)}), bf16[3,4096,512]{1,2,0:T(8,128)(2,1)}) %all-gather.6.cloned.1.call-update) | async-done | bytes 12582928 | tf_op jit(solution)/shard_map/all_gather | solution.py:88
  245.0 17.0 %fusion.27 = f32[3,1024,512]{1,2,0:T(8,128)S(1)} fusion(bf16[3,4096,512]{1,2,0:T(8,128)(2,1)} %all-gather.6.cloned.1.call-done, bf16[1024,4096]{1,0:T(8,128)(2,1)} %all-gather.8.cloned.1.call-done), kind=kOutput, calls=%fused_computation.39 | convolution fusion | flops 12884901888 | bytes 27262976 | tf_op jit(solution)/shard_map/td,cdn->ctn/dot_general | solution.py:85
  262.0 1.8 fusion.35
  263.9 2.8 squeeze.41
  266.7 2.8 copy.54
  269.4 4.0 %squeeze.42 = f32[2,512,4,128]{1,0,3,2:T(2,128)} reshape(f32[1,1024,512]{1,2,0:T(8,128)} %get-tuple-element.209) | data formatting | bytes 4194304 | tf_op jit(solution)/shard_map/squeeze | solution.py:91
  273.4 4.1 %copy.56 = f32[2,512,4,128]{3,1,2,0:T(8,128)} copy(f32[2,512,4,128]{1,0,3,2:T(2,128)} %squeeze.42) | data formatting | bytes 4194304 | tf_op jit(solution)/shard_map/squeeze | solution.py:91
  277.6 1.6 convert_element_type.24
  279.1 2.8 multiply_convert_fusion.2
  281.9 2.7 fusion.30
  287.1 16.0 %all-reduce = f32[32]{0:T(128)S(1)} all-reduce(f32[32]{0:T(128)S(1)} %exponential_dynamic-update-slice_fusion), channel_id=2, replica_groups=mesh['seq'=8,'fsdp'=4] {'seq'}, use_global_device_ids=true, to_apply=%add | all-reduce | flops 32 | bytes 256
  303.2 1.2 copy.59
  304.4 29.6 %all-gather.10.cloned.1.call-done = f32[32,128,128]{2,1,0:T(8,128)} async-done(((f32[4,128,128]{2,1,0:T(8,128)}), f32[32,128,128]{2,1,0:T(8,128)}) %all-gather.10.cloned.1.call-update) | async-done | bytes 2097168 | tf_op jit(solution)/shard_map/all_gather | solution.py:11
  334.0 6.8 %while.35 = (s32[]{:T(128)}, f32[4,128,128]{2,1,0:T(8,128)S(1)}, s32[]{:T(128)}, f32[8,4]{1,0:T(8,128)S(1)}, f32[8,4,128,128]{3,2,1,0:T(8,128)}, /*index=5*/s32[]{:T(128)}, s32[]{:T(128)}, s32[]{:T(128)}) while((s32[]{:T(128)}, f32[4,128,128]{2,1,0:T(8,128)S(1)}, s32[]{:T(128)}, f32[8,4]{1,0:T(8,128)S(1)}, f32[8,4,128,128]{3,2,1,0:T(8,128)}, ...), condition=%wide.region_7.8_spmd, body=%wide.region_6.7_spmd.sunk | while | flops 131077 | bytes 786607 | solution.py:19
  334.0 1.1 bitcast_add_fusion.4
  340.9 14.1 %while.36 = (s32[]{:T(128)}, bf16[2,512,4,128]{3,2,1,0:T(4,128)(2,1)}, bf16[2,512,4,128]{1,3,2,0:T(8,128)(2,1)}, f32[2,512,4]{1,2,0:T(4,128)S(1)}, bf16[2,512,4,...) while((s32[]{:T(128)}, ...), condition=%wide.region_12.13_spmd, body=%wide.region_8.12_spmd.sunk | while | flops 945817664 | bytes 9858489 | solution.py:94
  341.0 1.2 reduce-window.24
  342.7 3.1 fusion.46
  348.0 1.2 reduce-window.24
  349.8 3.1 fusion.46
  355.1 2.4 copy.75
  (85 shorter events, 15.5 us)
Async XLA Ops:
  6.5 1.4 copy-start.3
  6.5 61.7 %all-gather.8.cloned.1.call-start = ((), (), s32[]{:S(2)}) async-start(), calls=%async_computation.1 | async-start | bytes 10485760 | tf_op jit(solution)/shard_map/all_gather | solution.py:74
  7.3 2.4 copy-start.6
  7.3 237.7 %all-gather.6.cloned.1.call-start = ((), (), s32[]{:S(2)}) async-start(), calls=%async_computation | async-start | bytes 14155776 | tf_op jit(solution)/shard_map/all_gather | solution.py:88
  9.6 324.4 %all-gather.10.cloned.1.call-start = ((), (), s32[]{:S(2)}) async-start(), calls=%async_computation.2 | async-start | bytes 2359296 | tf_op jit(solution)/shard_map/all_gather | solution.py:11
  279.1 2.8 copy-start.1
  281.9 2.8 copy-start.4
  281.9 2.8 copy-start.5
  284.7 1.1 copy-start.7
  284.7 18.5 %copy-start.2 = (bf16[2,512,4,128]{1,0,3,2:T(2,128)(2,1)S(1)}, bf16[2,512,4,128]{1,0,3,2:T(2,128)(2,1)}, u32[]{:S(2)}) copy-start(bf16[2,512,4,128]{1,0,3,2:T(2,128)(2,1)} %convert_element_type.24) | copy-start | bytes 3145732
  285.1 0.7 copy-start
Sparse Core Ops, SparseCore 0:
  8.9 59.2 all-gather.7
  70.3 174.6 all-gather.5
  285.9 48.0 all-gather.9
where the time goes:
time: 365 us; the launch traced here: 364 us
  waiting for transfers between devices  262 us (72%)
  local copies, waits for them, and re-layouts  27.7 us (8%)
  matrix products  27.4 us (8%)
  other arithmetic  16.1 us (4%)
  blocking collectives  16 us (4%)
  between operations  13.9 us (4%)
    all_gather x1, waiting for transfers between devices, on_device(): lax.all_gather(projection, 'seq', axis=1, tiled=True)  177 us
    all_gather x1, waiting for transfers between devices, on_device(): features = lax.all_gather(tokens, 'fsdp', axis=1, tiled=True)  55.2 us
    all_gather x1, waiting for transfers between devices, entering(): gathered = jax.tree.map(lambda a: lax.all_gather(a, axis), part)  29.6 us
    dot_general x1, matrix products, on_device(): jnp.einsum('td,cdn->ctn', features, lax.all_gather(projection, 'seq', axi...  17 us
    unnamed x1, blocking collectives  16 us
    squeeze x2, local copies, waits for them, and re-layouts, on_device(): key_vecs, value_vecs, incoming = chain(raw[1], raw[2], decay, shaped)  8.14 us
  transfers between devices with their start and end apart: 3, of which 3 were waited for; matrix products, arithmetic and copies ran while one was open for 2% of the time, Pallas kernels for 0%

commit v1 on v0

v1 whole, which is shorter than its diff:
```python
import functools

import jax
import jax.numpy as jnp
from jax import lax
from jax.experimental import pallas as pl
from jax.experimental.pallas import tpu as pltpu
from jax.sharding import PartitionSpec as P

BLK = 512
HEAD = 128
PIECES = 4
MESH = pl.DeviceIdType.MESH
X, Y, D, C, CX, CY, CD = range(7)
F32 = jnp.float32
BF16 = jnp.bfloat16


def silu(v):
    return v / (1.0 + jnp.exp(-v))


def dot(a, b, dims=((1,), (0,))):
    return lax.dot_general(a, b, (dims, ((), ())), preferred_element_type=F32)


def split(v):
    high = v.astype(BF16)
    return high, (v - high.astype(F32)).astype(BF16)


def kernel(
    S,
    Fn,
    tok_in,
    proj_in,
    dec_in,
    out,
    tok,
    wts,
    dec,
    cols,
    fade,
    keys,
    vals,
    qry,
    before,
    own_state,
    s_in,
    s_out,
    done,
    tsend,
    trecv,
    wloc,
    wysend,
    wyrecv,
    wrsend,
    wlsend,
    wrecv,
    misc,
    osend,
    orecv,
    oloc,
):
    Z = S // 2
    s, f = lax.axis_index("seq"), lax.axis_index("fsdp")
    z, y = s // 2, s % 2
    x, c = f // 2, f % 2
    rows, kf = tok_in.shape
    ks = proj_in.shape[1]
    half = proj_in.shape[2] // 2
    heads = half // HEAD
    nb = rows // BLK
    depth = 2 * ks
    prow = rows // PIECES

    to_x = (s, (1 - x) * 2 + c)
    to_y = (z * 2 + 1 - y, f)
    to_c = (s, x * 2 + 1 - c)
    to_r = (jnp.minimum(z + 1, Z - 1) * 2 + y, f)
    to_l = (jnp.maximum(z - 1, 0) * 2 + y, f)
    has_l, has_r = z > 0, z < Z - 1

    def shard(yy, xx, cc):
        return yy * Fn + xx * 2 + cc

    place = {
        X: shard(y, 1 - x, c),
        Y: shard(1 - y, x, c),
        D: shard(1 - y, 1 - x, c),
        C: shard(y, x, 1 - c),
        CX: shard(y, 1 - x, 1 - c),
        CY: shard(1 - y, x, 1 - c),
        CD: shard(1 - y, 1 - x, 1 - c),
    }
    mine = shard(y, x, c)

    def remote(src, dst, ssem, rsem, to):
        return pltpu.make_async_remote_copy(
            src_ref=src, dst_ref=dst, send_sem=ssem, recv_sem=rsem, device_id=to, device_id_type=MESH
        )

    barrier = pltpu.get_barrier_semaphore()
    for to in (to_x, to_y, to_c):
        pl.semaphore_signal(barrier, inc=1, device_id=to, device_id_type=MESH)

    @pl.when(has_l)
    def _():
        pl.semaphore_signal(barrier, inc=1, device_id=to_l, device_id_type=MESH)

    @pl.when(has_r)
    def _():
        pl.semaphore_signal(barrier, inc=1, device_id=to_r, device_id_type=MESH)

    pl.semaphore_wait(barrier, 3 + (z + Z - 1) // Z + (2 * Z - 2 - z) // Z)

    def tcopy(kind, i, to, at, src=None):
        here = tok.at[at, pl.ds(i * prow, prow)]
        return remote(here if src is None else src, here, tsend.at[kind, i], trecv.at[kind, i], to)

    def own_tok(kind, i, to):
        return tcopy(kind, i, to, mine, tok_in.at[pl.ds(i * prow, prow)])

    def got_tok(kind, i):
        tcopy(kind, i, to_c, place[kind]).wait_recv()

    def via_y(i):
        return i == PIECES - 1

    def tok_step(i):
        got_tok(X, i)
        tcopy(CX, i, to_c, place[X]).start()
        if via_y(i):
            tcopy(D, i, to_y, place[X]).start()
        got_tok(Y, i)
        tcopy(CY, i, to_c, place[Y]).start()
        if not via_y(i):
            tcopy(D, i, to_x, place[Y]).start()

    def diag_step(i):
        got_tok(D, i)
        tcopy(CD, i, to_c, place[D]).start()

    parts = [(1, 0, half), (2, 0, half)]
    for h in range(heads):
        parts.append((0, h * HEAD, HEAD))

    def wslot(n, at):
        p, lo, width = parts[n]
        return wts.at[p, at, :, :, pl.ds(lo, width)]

    def wmember(n, yy):
        p, lo, width = parts[n]
        return wts.at[p, z, yy, :, pl.ds(lo, width)]

    def wsource(n, yy):
        p, lo, width = parts[n]
        return proj_in.at[p, :, pl.ds(pl.multiple_of(yy * half + lo, HEAD), width)]

    def wlocal(n):
        return pltpu.make_async_copy(wsource(n, y), wmember(n, y), wloc.at[n])

    def wpair(n):
        return remote(wsource(n, 1 - y), wmember(n, y), wysend.at[n], wyrecv.at[n], to_y)

    def wright(n, at):
        slot = wslot(n, at)
        return remote(slot, slot, wrsend.at[n, at], wrecv.at[n, at], to_r)

    def wleft(n, at):
        slot = wslot(n, at)
        return remote(slot, slot, wlsend.at[n, at], wrecv.at[n, at], to_l)

    def own_part(n):
        wlocal(n).wait()
        remote(wsource(n, y), wmember(n, 1 - y), wysend.at[n], wyrecv.at[n], to_y).wait_recv()

        @pl.when(has_r)
        def _():
            wright(n, z).start()

        @pl.when(has_l)
        def _():
            wleft(n, z).start()

    def wstep(n, d):
        @pl.when(z - d >= 0)
        def _():
            wright(n, z - d).wait_recv()

            @pl.when(has_r)
            def _():
                wright(n, z - d).start()

        @pl.when(z + d <= Z - 1)
        def _():
            wleft(n, z + d).wait_recv()

            @pl.when(has_l)
            def _():
                wleft(n, z + d).start()

    dec_copy = remote(dec_in.at[1 - y], dec.at[y], misc.at[0], misc.at[1], to_y)
    dec_copy.start()
    dec_local = pltpu.make_async_copy(dec_in.at[y], dec.at[y], misc.at[2])
    for n in (0, 1):
        wpair(n).start()
    for n in range(len(parts)):
        wlocal(n).start()
    for i in range(PIECES):
        own_tok(X, i, to_x).start()
        own_tok(Y, i, to_y).start()
        own_tok(C, i, to_c).start()
    for n in range(2, len(parts)):
        wpair(n).start()
    tok_local = pltpu.make_async_copy(tok_in, tok.at[mine], misc.at[3])
    tok_local.start()
    own_part(0)
    own_part(1)

    dec_local.start()
    dec_local.wait()
    remote(dec_in.at[y], dec.at[1 - y], misc.at[0], misc.at[1], to_y).wait_recv()
    lane = lax.broadcasted_iota(jnp.int32, (8, BLK), 1)
    for yy in range(2):
        run = dec[yy]
        step = 1
        while step < BLK:
            run = run + jnp.where(lane >= step, pltpu.roll(run, step, 1), 0.0)
            step *= 2
        dec[yy] = run
        cols[yy] = run.T
    for h in range(heads):
        for b in range(nb):
            at = h * nb + b

            def fading(yy, _, h=h, b=b, at=at):
                gap = cols[yy, :, at : at + 1] - dec[yy, at : at + 1, :]
                t = lax.broadcasted_iota(jnp.int32, (BLK, BLK), 0)
                u = lax.broadcasted_iota(jnp.int32, (BLK, BLK), 1)
                fade[h, yy * nb + b] = jnp.exp(jnp.where(t >= u, gap, -1e30))
                return 0

            lax.fori_loop(0, 2, fading, 0)

    def project(n, yy, store):
        p, lo, width = parts[n]

        def tile(i, _):
            r = pl.ds(pl.multiple_of(i * BLK, BLK), BLK)
            total = None
            for at in range(Z):
                ff, off = (at * depth) // kf, (at * depth) % kf
                w = wts[p, at, :, :, lo : lo + width].reshape(depth, width)
                part = dot(tok[yy * Fn + ff, r, off : off + depth], w)
                total = part if total is None else total + part
            store(pl.ds(pl.multiple_of(yy * rows + i * BLK, BLK), BLK), total)
            return 0

        lax.fori_loop(0, nb, tile, 0)

    def store_key(r, v):
        keys[r, :] = silu(v).astype(BF16)

    def store_val(r, v):
        vals[r, :] = v.astype(BF16)

    last = Z - 1
    early = [(0, d) for d in range(1, Z)] + [(1, 1)]
    per = -(-len(early) // PIECES)
    for i in range(PIECES):
        tok_step(i)
        for n, d in early[i * per : (i + 1) * per]:
            wstep(n, d)
    if heads > 0:
        own_part(2)
    for i in range(PIECES):
        got_tok(C, i)
        got_tok(CX, i)
    tok_local.wait()
    project(0, y, store_key)
    middle = [(1, d) for d in range(2, Z)]
    per = -(-len(middle) // 2)
    for i in range(2):
        for j in range(i * PIECES // 2, (i + 1) * PIECES // 2):
            diag_step(j)
        for n, d in middle[i * per : (i + 1) * per]:
            wstep(n, d)
    for n in range(3, len(parts)):
        own_part(n)
    project(1, y, store_val)
    wstep(2, 1)
    for i in range(PIECES):
        got_tok(CY, i)
        got_tok(CD, i)
    project(0, 1 - y, store_key)
    project(1, 1 - y, store_val)

    for h in range(heads):
        hc = slice(h * HEAD, (h + 1) * HEAD)
        state = jnp.zeros((HEAD, HEAD), F32)
        for j in range(2 * nb):
            yy, b = j // nb, j % nb
            at = h * nb + b
            before[h, j] = state
            run = cols[yy, :, at : at + 1]
            end = dec[yy, at : at + 1, BLK - 1 : BLK]
            r = slice(j * BLK, (j + 1) * BLK)
            carried = keys[r, hc].astype(F32) * jnp.exp(end - run)
            high, low = split(carried)
            v = vals[r, hc]
            fresh = dot(high, v, ((0,), (0,))) + dot(low, v, ((0,), (0,)))
            state = jnp.exp(end) * state + fresh
        own_state[h] = state

    for n in range(2, len(parts)):
        for d in range(1, Z):
            if (n, d) != (2, 1) and not (n == len(parts) - 1 and d == last):
                wstep(n, d)

    state_copy = remote(s_out, s_in, misc.at[4], misc.at[5], to_r)

    @pl.when(has_l)
    def _():
        state_copy.wait_recv()

    @pl.when(z == 0)
    def _():
        s_in[...] = jnp.zeros_like(s_in)

    for h in range(heads):
        lead = jnp.zeros((1, 1), F32)
        for j in range(2 * nb):
            yy, b = j // nb, j % nb
            at = h * nb + b
            before[h, j] = before[h, j] + jnp.exp(lead) * s_in[h]
            lead = lead + dec[yy, at : at + 1, BLK - 1 : BLK]
        s_out[h] = own_state[h] + jnp.exp(lead) * s_in[h]

    @pl.when(has_r)
    def _():
        state_copy.start()

    def place_out(h, b, who):
        return out.at[
            pl.ds(b * BLK, BLK), pl.ds(pl.multiple_of(who * half + h * HEAD, HEAD), HEAD)
        ]

    def give(h, b):
        src = done.at[h, (1 - y) * nb + b]
        return remote(src, place_out(h, b, y), osend.at[h, b], orecv.at[h, b], to_y)

    def keep(h, b):
        return pltpu.make_async_copy(done.at[h, y * nb + b], place_out(h, b, y), oloc.at[h, b])

    def attend(h, yy, b):
        at = h * nb + b
        j = yy * nb + b
        hc = slice(h * HEAD, (h + 1) * HEAD)
        r = pl.ds(pl.multiple_of(j * BLK, BLK), BLK)
        q, k, v = qry[r, :], keys[r, hc], vals[r, hc]
        scores = dot(q, k, ((1,), (1,)))
        weights = (fade[h, j] * scores).astype(BF16)
        high, low = split(before[h, j])
        inter = dot(q, jnp.concatenate([high, low], axis=1))
        inter = inter[:, :HEAD] + inter[:, HEAD:]
        mixed = dot(weights, v) + jnp.exp(cols[yy, :, at : at + 1]) * inter
        scale = lax.rsqrt(jnp.mean(mixed * mixed, axis=-1, keepdims=True) + 1e-6)
        done[h, j] = (mixed * scale).astype(BF16)

    def store_query(r, v):
        qry[r, :] = silu(v).astype(BF16)

    for h in range(heads):
        if h == heads - 1:
            wstep(2 + h, last)
        project(2 + h, 1 - y, store_query)
        for b in range(nb):
            attend(h, 1 - y, b)
            give(h, b).start()
        project(2 + h, y, store_query)
        for b in range(nb):
            attend(h, y, b)
            keep(h, b).start()

    for h in range(heads):
        for b in range(nb):
            keep(h, b).wait()
            give(h, b).wait_send()
            remote(
                done.at[h, y * nb + b],
                place_out(h, b, 1 - y),
                osend.at[h, b],
                orecv.at[h, b],
                to_y,
            ).wait_recv()

    @pl.when(has_r)
    def _():
        state_copy.wait_send()

    dec_copy.wait_send()
    for n in range(len(parts)):
        wpair(n).wait_send()
        for at in range(Z):

            @pl.when(has_r & (at <= z))
            def _():
                wright(n, at).wait_send()

            @pl.when(has_l & (at >= z))
            def _():
                wleft(n, at).wait_send()

    for i in range(PIECES):
        own_tok(X, i, to_x).wait_send()
        own_tok(Y, i, to_y).wait_send()
        own_tok(C, i, to_c).wait_send()
        tcopy(CX, i, to_c, place[X]).wait_send()
        tcopy(CY, i, to_c, place[Y]).wait_send()
        tcopy(CD, i, to_c, place[D]).wait_send()
        if via_y(i):
            tcopy(D, i, to_y, place[X]).wait_send()
        else:
            tcopy(D, i, to_x, place[Y]).wait_send()


def on_device(S, Fn, tokens, projection, log_decay):
    rows, kf = tokens.shape
    ks, width = projection.shape[1:]
    Z = S // 2
    half = width // 2
    heads = half // HEAD
    nb = rows // BLK
    parts = 2 + heads
    dec = log_decay.T.reshape(2, heads * nb, BLK)
    dec = jnp.pad(dec, ((0, 0), (0, 8 - heads * nb), (0, 0)))
    dma = pltpu.SemaphoreType.DMA
    any_spec = pl.BlockSpec(memory_space=pl.ANY)
    return pl.pallas_call(
        functools.partial(kernel, S, Fn),
        out_shape=jax.ShapeDtypeStruct((rows, width), BF16),
        in_specs=[any_spec] * 3,
        out_specs=any_spec,
        scratch_shapes=[
            pltpu.VMEM((2 * Fn, rows, kf), BF16),
            pltpu.VMEM((3, Z, 2, ks, half), BF16),
            pltpu.VMEM((2, 8, BLK), F32),
            pltpu.VMEM((2, BLK, 8), F32),
            pltpu.VMEM((heads, 2 * nb, BLK, BLK), F32),
            pltpu.VMEM((2 * rows, half), BF16),
            pltpu.VMEM((2 * rows, half), BF16),
            pltpu.VMEM((2 * rows, HEAD), BF16),
            pltpu.VMEM((heads, 2 * nb, HEAD, HEAD), F32),
            pltpu.VMEM((heads, HEAD, HEAD), F32),
            pltpu.VMEM((heads, HEAD, HEAD), F32),
            pltpu.VMEM((heads, HEAD, HEAD), F32),
            pltpu.VMEM((heads, 2 * nb, BLK, HEAD), BF16),
            dma((7, PIECES)),
            dma((7, PIECES)),
            dma((parts,)),
            dma((parts,)),
            dma((parts,)),
            dma((parts, Z)),
            dma((parts, Z)),
            dma((parts, Z)),
            dma((6,)),
            dma((heads, nb)),
            dma((heads, nb)),
            dma((heads, nb)),
        ],
        compiler_params=pltpu.CompilerParams(
            collective_id=0, has_side_effects=True, vmem_limit_bytes=52 * 1024 * 1024
        ),
    )(tokens, projection, dec)


def solution(mesh):
    S, Fn = mesh.shape["seq"], mesh.shape["fsdp"]
    return jax.shard_map(
        functools.partial(on_device, S, Fn),
        mesh=mesh,
        in_specs=(P("seq", "fsdp"), P(None, "seq", "fsdp"), P("seq", "fsdp")),
        out_specs=P("seq", "fsdp"),
        check_vma=False,
    )
```

time: 365 us -> 146 us (0.40)
  waiting for transfers between devices: 262 us -> 0 us
  Pallas kernels: 0 us -> 144 us
  matrix products: 27.4 us -> 0 us
  local copies, waits for them, and re-layouts: 27.7 us -> 1.72 us
  other arithmetic: 16.1 us -> 0 us
  blocking collectives: 16 us -> 0 us
  between operations: 13.9 us -> 0.02 us
    all_gather x3 -> x0, waiting for transfers between devices: 262 us -> none  [the longest x1 177 us: on_device(): lax.all_gather(projection, 'seq', axis=1, tiled=True)]
    pallas_call x0 -> x1, Pallas kernels: none -> 144 us  [on_device(): pl.pallas_call(functools.partial(kernel, S, Fn), out_shape=jax.ShapeDtype...]
    dot_general x6 -> x0, matrix products: 27.4 us -> none  [the longest x1 17 us: on_device(): jnp.einsum('td,cdn->ctn', features, lax.all_gather(projection, 'seq', axi...]
    unnamed x1 -> x0, blocking collectives: 16 us -> none
    squeeze x4 -> x0, local copies, waits for them, and re-layouts: 13.7 us -> none  [the longest x2 8.14 us: on_device(): key_vecs, value_vecs, incoming = chain(raw[1], raw[2], decay, shaped)]
    add x9 -> x0, other arithmetic: 6.67 us -> none  [the longest x6 6.37 us: combine(): later[0][:, None, None] * earlier[1] + later[1]]
    another operation x8 -> x0, other arithmetic: 5.71 us -> none
    unnamed x21 -> x1, local copies, waits for them, and re-layouts: 6.01 us -> 0.97 us
  transfers between devices with their start and end apart: 3 -> 0, of which waited for: 3 -> 0; matrix products, arithmetic and copies ran while one was open for 2% -> 0% of each run, Pallas kernels for 0% -> 0%
where the time goes in v1:
time: 146 us; the launch traced here: 145 us
  Pallas kernels  144 us (99%)
  local copies, waits for them, and re-layouts  1.72 us (1%)
    pallas_call x1, Pallas kernels, on_device(): pl.pallas_call(functools.partial(kernel, S, Fn), out_shape=jax.ShapeDtype...  144 us

profile of v1, /device:TPU:24, one launch (start us, length us, event | category | flops | bytes accessed | tf_op | source)
XLA Modules:
  0.0 145.4 jit_solution(16472113176879110909)
XLA Ops:
  0.0 0.7 reshape.3
  0.8 143.7 %shard_map.37 = bf16[1024,512]{1,0:T(8,128)(2,1)S(1)} custom-call(bf16[1024,1024]{1,0:T(8,128)(2,1)} %tok_in.1, bf16[3,512,512]{2,1,0:T(8,128)(2,1)} %proj_in.1, f32[2,8,512]{2,1,0:T(8,128)S(1)} %pad.4.dec_in), custom_call_target="tpu_custom_call" | custom-call | tf_op jit(solution)/shard_map/pallas_call | solution.py:440
  144.4 1.0 copy.5
  (1 shorter events, 0.0 us)

commit v2 on v1

--- a/solution.py
+++ b/solution.py
@@ -10,6 +10,7 @@
 BLK = 512
 HEAD = 128
 PIECES = 4
+AHEAD = 2
 MESH = pl.DeviceIdType.MESH
 X, Y, D, C, CX, CY, CD = range(7)
 F32 = jnp.float32
@@ -43,9 +44,9 @@
     fade,
     keys,
     vals,
-    qry,
+    qacc,
+    fresh,
     before,
-    own_state,
     s_in,
     s_out,
     done,
@@ -127,15 +128,21 @@
     def via_y(i):
         return i == PIECES - 1
 
-    def tok_step(i):
+    def side_step(i):
         got_tok(X, i)
         tcopy(CX, i, to_c, place[X]).start()
         if via_y(i):
             tcopy(D, i, to_y, place[X]).start()
+        if i + AHEAD < PIECES:
+            own_tok(X, i + AHEAD, to_x).start()
+
+    def pair_step(i):
         got_tok(Y, i)
         tcopy(CY, i, to_c, place[Y]).start()
         if not via_y(i):
             tcopy(D, i, to_x, place[Y]).start()
+        if i + AHEAD < PIECES:
+            own_tok(Y, i + AHEAD, to_y).start()
 
     def diag_step(i):
         got_tok(D, i)
@@ -199,20 +206,25 @@
             @pl.when(has_l)
             def _():
                 wleft(n, z + d).start()
+
+    def wsteps(n, i, slots=3):
+        for d in range(1 + i * (Z - 1) // slots, 1 + (i + 1) * (Z - 1) // slots):
+            wstep(n, d)
 
     dec_copy = remote(dec_in.at[1 - y], dec.at[y], misc.at[0], misc.at[1], to_y)
     dec_copy.start()
     dec_local = pltpu.make_async_copy(dec_in.at[y], dec.at[y], misc.at[2])
     for n in (0, 1):
         wpair(n).start()
-    for n in range(len(parts)):
+    for n in range(2):
         wlocal(n).start()
-    for i in range(PIECES):
+    for i in range(AHEAD):
         own_tok(X, i, to_x).start()
         own_tok(Y, i, to_y).start()
+    for i in range(PIECES):
         own_tok(C, i, to_c).start()
     for n in range(2, len(parts)):
-        wpair(n).start()
+        wlocal(n).start()
     tok_local = pltpu.make_async_copy(tok_in, tok.at[mine], misc.at[3])
     tok_local.start()
     own_part(0)
@@ -243,103 +255,160 @@
 
             lax.fori_loop(0, 2, fading, 0)
 
-    def project(n, yy, store):
+    def chunk(n, yy, r, at):
         p, lo, width = parts[n]
-
+        w = wts[p, at, :, :, lo : lo + width].reshape(depth, width)
+        ff, off = (at * depth) // kf, (at * depth) % kf
+        if depth == kf:
+            return dot(tok[yy * Fn + ff, r, :], w)
+        if not isinstance(at, int):
+            off = pl.multiple_of(off, HEAD)
+        return dot(tok[yy * Fn + ff, r, pl.ds(off, depth)], w)
+
+    def project(n, yy, i):
+        r = pl.ds(i * BLK, BLK)
+        total = chunk(n, yy, r, 0)
+        for at in range(1, Z):
+            total = total + chunk(n, yy, r, at)
+        to = pl.ds(pl.multiple_of(yy * rows + i * BLK, BLK), BLK)
+        if n == 0:
+            keys[to, :] = silu(total).astype(BF16)
+        else:
+            vals[to, :] = total.astype(BF16)
+
+    def states(yy, b):
+        j = yy * nb + b
+        r = pl.ds(pl.multiple_of(j * BLK, BLK), BLK)
+        for h in range(heads):
+            hc = slice(h * HEAD, (h + 1) * HEAD)
+            at = h * nb + b
+            run = cols[yy, :, at : at + 1]
+            end = dec[yy, at : at + 1, BLK - 1 : BLK]
+            high, low = split(keys[r, hc].astype(F32) * jnp.exp(end - run))
+            v = vals[r, hc]
+            fresh[h, j] = dot(high, v, ((0,), (0,))) + dot(low, v, ((0,), (0,)))
+
+    def got_core(kinds, i):
+        lo, hi = i * PIECES // nb, (i + 1) * PIECES // nb
+        for j in range(lo, hi):
+            for kind in kinds:
+                got_tok(kind, j)
+
+    near = (z // (Z - 1)) * (Z - 1)
+    far = Z - 1 - near
+
+    def begin_query(h):
         def tile(i, _):
-            r = pl.ds(pl.multiple_of(i * BLK, BLK), BLK)
-            total = None
-            for at in range(Z):
-                ff, off = (at * depth) // kf, (at * depth) % kf
-                w = wts[p, at, :, :, lo : lo + width].reshape(depth, width)
-                part = dot(tok[yy * Fn + ff, r, off : off + depth], w)
-                total = part if total is None else total + part
-            store(pl.ds(pl.multiple_of(yy * rows + i * BLK, BLK), BLK), total)
+            yy, b = i // nb, i % nb
+            r = pl.ds(pl.multiple_of(b * BLK, BLK), BLK)
+            total = chunk(2 + h, yy, r, near)
+            for at in range(1, Z - 1):
+                total = total + chunk(2 + h, yy, r, at)
+            qacc[h, pl.ds(pl.multiple_of(i * BLK, BLK), BLK), :] = total
             return 0
 
-        lax.fori_loop(0, nb, tile, 0)
-
-    def store_key(r, v):
-        keys[r, :] = silu(v).astype(BF16)
-
-    def store_val(r, v):
-        vals[r, :] = v.astype(BF16)
-
-    last = Z - 1
-    early = [(0, d) for d in range(1, Z)] + [(1, 1)]
-    per = -(-len(early) // PIECES)
-    for i in range(PIECES):
-        tok_step(i)
-        for n, d in early[i * per : (i + 1) * per]:
-            wstep(n, d)
-    if heads > 0:
-        own_part(2)
-    for i in range(PIECES):
-        got_tok(C, i)
-        got_tok(CX, i)
+        lax.fori_loop(0, 2 * nb, tile, 0)
+
+    side_step(0)
+    wsteps(0, 0)
+    pair_step(0)
+    side_step(1)
+    wsteps(0, 1)
+    pair_step(1)
+    for n in range(2, len(parts)):
+        wpair(n).start()
+    for i in range(2, PIECES):
+        side_step(i)
+        if i == 2:
+            wsteps(0, 2)
+            pair_step(2)
+    own_part(2)
+    wsteps(1, 0)
     tok_local.wait()
-    project(0, y, store_key)
-    middle = [(1, d) for d in range(2, Z)]
-    per = -(-len(middle) // 2)
-    for i in range(2):
-        for j in range(i * PIECES // 2, (i + 1) * PIECES // 2):
-            diag_step(j)
-        for n, d in middle[i * per : (i + 1) * per]:
-            wstep(n, d)
+    got_core((C, CX), 0)
+    project(0, y, 0)
+    for i in range(3, PIECES):
+        pair_step(i)
+    wsteps(1, 1)
+    for i in range(1, nb):
+        got_core((C, CX), i)
+        project(0, y, i)
+    diag_step(0)
+    wsteps(1, 2)
     for n in range(3, len(parts)):
         own_part(n)
-    project(1, y, store_val)
-    wstep(2, 1)
-    for i in range(PIECES):
-        got_tok(CY, i)
-        got_tok(CD, i)
-    project(0, 1 - y, store_key)
-    project(1, 1 - y, store_val)
-
-    for h in range(heads):
-        hc = slice(h * HEAD, (h + 1) * HEAD)
-        state = jnp.zeros((HEAD, HEAD), F32)
-        for j in range(2 * nb):
-            yy, b = j // nb, j % nb
-            at = h * nb + b
-            before[h, j] = state
-            run = cols[yy, :, at : at + 1]
-            end = dec[yy, at : at + 1, BLK - 1 : BLK]
-            r = slice(j * BLK, (j + 1) * BLK)
-            carried = keys[r, hc].astype(F32) * jnp.exp(end - run)
-            high, low = split(carried)
-            v = vals[r, hc]
-            fresh = dot(high, v, ((0,), (0,))) + dot(low, v, ((0,), (0,)))
-            state = jnp.exp(end) * state + fresh
-        own_state[h] = state
-
-    for n in range(2, len(parts)):
-        for d in range(1, Z):
-            if (n, d) != (2, 1) and not (n == len(parts) - 1 and d == last):
-                wstep(n, d)
+    project(1, y, 0)
+    diag_step(PIECES - 1)
+    for i in range(1, PIECES // nb):
+        diag_step(i)
+    for i in range(1, nb):
+        project(1, y, i)
+    wsteps(2, 0)
+    got_core((CY, CD), 0)
+    project(0, 1 - y, 0)
+    project(1, 1 - y, 0)
+    wsteps(2, 1)
+    for b in range(nb):
+        states(y, b)
+    states(1 - y, 0)
+    for i in range(PIECES // nb, PIECES - 1):
+        diag_step(i)
+    for i in range(1, nb):
+        got_core((CY, CD), i)
+        project(0, 1 - y, i)
+        project(1, 1 - y, i)
+        states(1 - y, i)
 
     state_copy = remote(s_out, s_in, misc.at[4], misc.at[5], to_r)
 
-    @pl.when(has_l)
+    def chain():
+        for h in range(heads):
+            state = jnp.zeros((HEAD, HEAD), F32)
+            lead = jnp.zeros((1, 1), F32)
+            for j in range(2 * nb):
+                yy, at = j // nb, h * nb + j % nb
+                end = dec[yy, at : at + 1, BLK - 1 : BLK]
+                before[h, j] = state
+                state = jnp.exp(end) * state + fresh[h, j]
+                lead = lead + end
+            s_out[h] = state
+
+        @pl.when(has_l)
+        def _():
+            state_copy.wait_recv()
+            for h in range(heads):
+                lead = jnp.zeros((1, 1), F32)
+                for j in range(2 * nb):
+                    yy, at = j // nb, h * nb + j % nb
+                    lead = lead + dec[yy, at : at + 1, BLK - 1 : BLK]
+                s_out[h] = s_out[h] + jnp.exp(lead) * s_in[h]
+
+        @pl.when(has_r)
+        def _():
+            state_copy.start()
+
+        @pl.when(has_l)
+        def _():
+            for h in range(heads):
+                lead = jnp.zeros((1, 1), F32)
+                for j in range(2 * nb):
+                    yy, at = j // nb, h * nb + j % nb
+                    before[h, j] = before[h, j] + jnp.exp(lead) * s_in[h]
+                    lead = lead + dec[yy, at : at + 1, BLK - 1 : BLK]
+
+    @pl.when(z < Z // 2)
     def _():
-        state_copy.wait_recv()
-
-    @pl.when(z == 0)
+        chain()
+
+    wsteps(2, 2)
+    begin_query(0)
+    for n in range(3, len(parts)):
+        for d in range(1, Z - 1):
+            wstep(n, d)
+
+    @pl.when(z >= Z // 2)
     def _():
-        s_in[...] = jnp.zeros_like(s_in)
-
-    for h in range(heads):
-        lead = jnp.zeros((1, 1), F32)
-        for j in range(2 * nb):
-            yy, b = j // nb, j % nb
-            at = h * nb + b
-            before[h, j] = before[h, j] + jnp.exp(lead) * s_in[h]
-            lead = lead + dec[yy, at : at + 1, BLK - 1 : BLK]
-        s_out[h] = own_state[h] + jnp.exp(lead) * s_in[h]
-
-    @pl.when(has_r)
-    def _():
-        state_copy.start()
+        chain()
 
     def place_out(h, b, who):
         return out.at[
@@ -358,7 +427,8 @@
         j = yy * nb + b
         hc = slice(h * HEAD, (h + 1) * HEAD)
         r = pl.ds(pl.multiple_of(j * BLK, BLK), BLK)
-        q, k, v = qry[r, :], keys[r, hc], vals[r, hc]
+        total = qacc[h, r, :] + chunk(2 + h, yy, pl.ds(b * BLK, BLK), far)
+        q, k, v = silu(total).astype(BF16), keys[r, hc], vals[r, hc]
         scores = dot(q, k, ((1,), (1,)))
         weights = (fade[h, j] * scores).astype(BF16)
         high, low = split(before[h, j])
@@ -368,17 +438,14 @@
         scale = lax.rsqrt(jnp.mean(mixed * mixed, axis=-1, keepdims=True) + 1e-6)
         done[h, j] = (mixed * scale).astype(BF16)
 
-    def store_query(r, v):
-        qry[r, :] = silu(v).astype(BF16)
-
     for h in range(heads):
-        if h == heads - 1:
-            wstep(2 + h, last)
-        project(2 + h, 1 - y, store_query)
+        if h > 0:
+            wstep(2 + h, Z - 1)
         for b in range(nb):
             attend(h, 1 - y, b)
             give(h, b).start()
-        project(2 + h, y, store_query)
+        if h + 1 < heads:
+            begin_query(h + 1)
         for b in range(nb):
             attend(h, y, b)
             keep(h, b).start()
@@ -450,9 +517,9 @@
             pltpu.VMEM((heads, 2 * nb, BLK, BLK), F32),
             pltpu.VMEM((2 * rows, half), BF16),
             pltpu.VMEM((2 * rows, half), BF16),
-            pltpu.VMEM((2 * rows, HEAD), BF16),
+            pltpu.VMEM((heads, 2 * rows, HEAD), F32),
             pltpu.VMEM((heads, 2 * nb, HEAD, HEAD), F32),
-            pltpu.VMEM((heads, HEAD, HEAD), F32),
+            pltpu.VMEM((heads, 2 * nb, HEAD, HEAD), F32),
             pltpu.VMEM((heads, HEAD, HEAD), F32),
             pltpu.VMEM((heads, HEAD, HEAD), F32),
             pltpu.VMEM((heads, 2 * nb, BLK, HEAD), BF16),

time: 146 us -> 156 us (1.068)
  Pallas kernels: 144 us -> 154 us
    pallas_call x1, Pallas kernels: 144 us -> 154 us  [on_device(): pl.pallas_call(functools.partial(kernel, S, Fn), out_shape=jax.ShapeDtype...]
where the time goes in v2:
time: 156 us; the launch traced here: 155 us
  Pallas kernels  154 us (99%)
  local copies, waits for them, and re-layouts  1.72 us (1%)
    pallas_call x1, Pallas kernels, on_device(): pl.pallas_call(functools.partial(kernel, S, Fn), out_shape=jax.ShapeDtype...  154 us

profile of v2, /device:TPU:24, one launch (start us, length us, event | category | flops | bytes accessed | tf_op | source)
XLA Modules:
  0.0 155.5 jit_solution(3347236363189177087)
XLA Ops:
  0.0 0.7 reshape.3
  0.8 153.8 %shard_map.37 = bf16[1024,512]{1,0:T(8,128)(2,1)S(1)} custom-call(bf16[1024,1024]{1,0:T(8,128)(2,1)} %tok_in.1, bf16[3,512,512]{2,1,0:T(8,128)(2,1)} %proj_in.1, f32[2,8,512]{2,1,0:T(8,128)S(1)} %pad.4.dec_in), custom_call_target="tpu_custom_call" | custom-call | tf_op jit(solution)/shard_map/pallas_call | solution.py:507
  154.5 1.0 copy.5
  (1 shorter events, 0.0 us)

commit v3 on v2

--- a/solution.py
+++ b/solution.py
@@ -10,7 +10,6 @@
 BLK = 512
 HEAD = 128
 PIECES = 4
-AHEAD = 2
 MESH = pl.DeviceIdType.MESH
 X, Y, D, C, CX, CY, CD = range(7)
 F32 = jnp.float32
@@ -47,6 +46,8 @@
     qacc,
     fresh,
     before,
+    kvacc,
+    enter,
     s_in,
     s_out,
     done,
@@ -59,6 +60,8 @@
     wlsend,
     wrecv,
     misc,
+    ssend,
+    srecv,
     osend,
     orecv,
     oloc,
@@ -105,15 +108,13 @@
     for to in (to_x, to_y, to_c):
         pl.semaphore_signal(barrier, inc=1, device_id=to, device_id_type=MESH)
 
-    @pl.when(has_l)
-    def _():
-        pl.semaphore_signal(barrier, inc=1, device_id=to_l, device_id_type=MESH)
-
-    @pl.when(has_r)
-    def _():
-        pl.semaphore_signal(barrier, inc=1, device_id=to_r, device_id_type=MESH)
-
-    pl.semaphore_wait(barrier, 3 + (z + Z - 1) // Z + (2 * Z - 2 - z) // Z)
+    for at in range(Z):
+
+        @pl.when(at != z)
+        def _(at=at):
+            pl.semaphore_signal(barrier, inc=1, device_id=(at * 2 + y, f), device_id_type=MESH)
+
+    pl.semaphore_wait(barrier, 3 + Z - 1)
 
     def tcopy(kind, i, to, at, src=None):
         here = tok.at[at, pl.ds(i * prow, prow)]
@@ -133,16 +134,12 @@
         tcopy(CX, i, to_c, place[X]).start()
         if via_y(i):
             tcopy(D, i, to_y, place[X]).start()
-        if i + AHEAD < PIECES:
-            own_tok(X, i + AHEAD, to_x).start()
 
     def pair_step(i):
         got_tok(Y, i)
         tcopy(CY, i, to_c, place[Y]).start()
         if not via_y(i):
             tcopy(D, i, to_x, place[Y]).start()
-        if i + AHEAD < PIECES:
-            own_tok(Y, i + AHEAD, to_y).start()
 
     def diag_step(i):
         got_tok(D, i)
@@ -207,8 +204,35 @@
             def _():
                 wleft(n, z + d).start()
 
-    def wsteps(n, i, slots=3):
-        for d in range(1 + i * (Z - 1) // slots, 1 + (i + 1) * (Z - 1) // slots):
+    def wdirect(n, to):
+        slot = wslot(n, z)
+        return remote(slot, slot, wrsend.at[n, to], wrecv.at[n, z], (to * 2 + y, f))
+
+    def own_query(n):
+        wlocal(n).wait()
+        remote(wsource(n, y), wmember(n, 1 - y), wysend.at[n], wyrecv.at[n], to_y).wait_recv()
+        for to in range(Z):
+
+            @pl.when(to != z)
+            def _(to=to):
+                wdirect(n, to).start()
+
+    near = (z // (Z - 1)) * (Z - 1)
+    far = Z - 1 - near
+
+    def got_query(n, at):
+        @pl.when(at != z)
+        def _():
+            wright(n, at).wait_recv()
+
+    def got_near(n):
+        got_query(n, near)
+        for at in range(1, Z - 1):
+            got_query(n, at)
+
+    def wsteps(n, i):
+        ends = (1, Z // 2, Z - 1, Z)
+        for d in range(ends[i], ends[i + 1]):
             wstep(n, d)
 
     dec_copy = remote(dec_in.at[1 - y], dec.at[y], misc.at[0], misc.at[1], to_y)
@@ -218,7 +242,7 @@
         wpair(n).start()
     for n in range(2):
         wlocal(n).start()
-    for i in range(AHEAD):
+    for i in range(PIECES):
         own_tok(X, i, to_x).start()
         own_tok(Y, i, to_y).start()
     for i in range(PIECES):
@@ -265,16 +289,26 @@
             off = pl.multiple_of(off, HEAD)
         return dot(tok[yy * Fn + ff, r, pl.ds(off, depth)], w)
 
-    def project(n, yy, i):
-        r = pl.ds(i * BLK, BLK)
-        total = chunk(n, yy, r, 0)
-        for at in range(1, Z):
+    def partial(n, yy, r):
+        total = chunk(n, yy, r, near)
+        for at in range(1, Z - 1):
             total = total + chunk(n, yy, r, at)
+        return total
+
+    def begin(n, i):
+        r = slice(i * BLK, (i + 1) * BLK)
+        kvacc[n, r, :] = partial(n, y, pl.ds(i * BLK, BLK))
+
+    def finish(n, yy, i, total):
+        total = total + chunk(n, yy, pl.ds(i * BLK, BLK), far)
         to = pl.ds(pl.multiple_of(yy * rows + i * BLK, BLK), BLK)
         if n == 0:
             keys[to, :] = silu(total).astype(BF16)
         else:
             vals[to, :] = total.astype(BF16)
+
+    def project(n, yy, i):
+        finish(n, yy, i, partial(n, yy, pl.ds(i * BLK, BLK)))
 
     def states(yy, b):
         j = yy * nb + b
@@ -294,121 +328,102 @@
             for kind in kinds:
                 got_tok(kind, j)
 
-    near = (z // (Z - 1)) * (Z - 1)
-    far = Z - 1 - near
-
     def begin_query(h):
         def tile(i, _):
             yy, b = i // nb, i % nb
             r = pl.ds(pl.multiple_of(b * BLK, BLK), BLK)
-            total = chunk(2 + h, yy, r, near)
-            for at in range(1, Z - 1):
-                total = total + chunk(2 + h, yy, r, at)
-            qacc[h, pl.ds(pl.multiple_of(i * BLK, BLK), BLK), :] = total
+            qacc[h, pl.ds(pl.multiple_of(i * BLK, BLK), BLK), :] = partial(2 + h, yy, r)
             return 0
 
         lax.fori_loop(0, 2 * nb, tile, 0)
 
     side_step(0)
+    pair_step(0)
     wsteps(0, 0)
-    pair_step(0)
-    side_step(1)
-    wsteps(0, 1)
-    pair_step(1)
+    wsteps(1, 0)
     for n in range(2, len(parts)):
         wpair(n).start()
-    for i in range(2, PIECES):
+    for i in range(1, PIECES - 1):
         side_step(i)
-        if i == 2:
-            wsteps(0, 2)
-            pair_step(2)
-    own_part(2)
-    wsteps(1, 0)
+        pair_step(i)
+    side_step(PIECES - 1)
+    wsteps(0, 1)
+    wsteps(1, 1)
+    pair_step(PIECES - 1)
+    for n in range(2, len(parts)):
+        own_query(n)
     tok_local.wait()
-    got_core((C, CX), 0)
-    project(0, y, 0)
-    for i in range(3, PIECES):
-        pair_step(i)
-    wsteps(1, 1)
-    for i in range(1, nb):
+    for i in range(nb):
         got_core((C, CX), i)
-        project(0, y, i)
-    diag_step(0)
-    wsteps(1, 2)
-    for n in range(3, len(parts)):
-        own_part(n)
-    project(1, y, 0)
-    diag_step(PIECES - 1)
+        begin(0, i)
+        begin(1, i)
+        if i == 0:
+            diag_step(0)
     for i in range(1, PIECES // nb):
         diag_step(i)
-    for i in range(1, nb):
-        project(1, y, i)
-    wsteps(2, 0)
+    diag_step(PIECES - 1)
+    wsteps(0, 2)
+    wsteps(1, 2)
+    for i in range(nb):
+        finish(0, y, i, kvacc[0, i * BLK : (i + 1) * BLK, :])
+        finish(1, y, i, kvacc[1, i * BLK : (i + 1) * BLK, :])
     got_core((CY, CD), 0)
     project(0, 1 - y, 0)
     project(1, 1 - y, 0)
-    wsteps(2, 1)
+    for i in range(PIECES // nb, PIECES - 1):
+        diag_step(i)
     for b in range(nb):
         states(y, b)
     states(1 - y, 0)
-    for i in range(PIECES // nb, PIECES - 1):
-        diag_step(i)
     for i in range(1, nb):
         got_core((CY, CD), i)
         project(0, 1 - y, i)
         project(1, 1 - y, i)
         states(1 - y, i)
 
-    state_copy = remote(s_out, s_in, misc.at[4], misc.at[5], to_r)
-
-    def chain():
-        for h in range(heads):
-            state = jnp.zeros((HEAD, HEAD), F32)
-            lead = jnp.zeros((1, 1), F32)
-            for j in range(2 * nb):
-                yy, at = j // nb, h * nb + j % nb
-                end = dec[yy, at : at + 1, BLK - 1 : BLK]
-                before[h, j] = state
-                state = jnp.exp(end) * state + fresh[h, j]
-                lead = lead + end
-            s_out[h] = state
-
-        @pl.when(has_l)
-        def _():
-            state_copy.wait_recv()
+    def state_copy(to):
+        return remote(
+            s_out, s_in.at[z], ssend.at[to], srecv.at[z], (to * 2 + y, f)
+        )
+
+    def block_end(h, j):
+        at = h * nb + j % nb
+        return dec[j // nb, at : at + 1, BLK - 1 : BLK]
+
+    for h in range(heads):
+        state = jnp.zeros((HEAD, HEAD), F32)
+        lead = jnp.zeros((1, 1), F32)
+        for j in range(2 * nb):
+            before[h, j] = state
+            state = jnp.exp(block_end(h, j)) * state + fresh[h, j]
+            lead = lead + block_end(h, j)
+        s_out[h, 0:HEAD, :] = state
+        s_out[h, HEAD : HEAD + 8, :] = jnp.broadcast_to(lead, (8, HEAD))
+    for to in range(1, Z):
+
+        @pl.when(to > z)
+        def _(to=to):
+            state_copy(to).start()
+
+    for h in range(heads):
+        got_near(2 + h)
+        begin_query(h)
+
+    enter[...] = jnp.zeros_like(enter)
+    for at in range(Z - 1):
+
+        @pl.when(at < z)
+        def _(at=at):
+            remote(s_out, s_in.at[at], ssend.at[at], srecv.at[at], (at * 2 + y, f)).wait_recv()
             for h in range(heads):
-                lead = jnp.zeros((1, 1), F32)
-                for j in range(2 * nb):
-                    yy, at = j // nb, h * nb + j % nb
-                    lead = lead + dec[yy, at : at + 1, BLK - 1 : BLK]
-                s_out[h] = s_out[h] + jnp.exp(lead) * s_in[h]
-
-        @pl.when(has_r)
-        def _():
-            state_copy.start()
-
-        @pl.when(has_l)
-        def _():
-            for h in range(heads):
-                lead = jnp.zeros((1, 1), F32)
-                for j in range(2 * nb):
-                    yy, at = j // nb, h * nb + j % nb
-                    before[h, j] = before[h, j] + jnp.exp(lead) * s_in[h]
-                    lead = lead + dec[yy, at : at + 1, BLK - 1 : BLK]
-
-    @pl.when(z < Z // 2)
-    def _():
-        chain()
-
-    wsteps(2, 2)
-    begin_query(0)
-    for n in range(3, len(parts)):
-        for d in range(1, Z - 1):
-            wstep(n, d)
-
-    @pl.when(z >= Z // 2)
-    def _():
-        chain()
+                decay = jnp.exp(s_in[at, h, HEAD : HEAD + 1, :])
+                enter[h] = decay * enter[h] + s_in[at, h, 0:HEAD, :]
+
+    for h in range(heads):
+        lead = jnp.zeros((1, 1), F32)
+        for j in range(2 * nb):
+            before[h, j] = before[h, j] + jnp.exp(lead) * enter[h]
+            lead = lead + block_end(h, j)
 
     def place_out(h, b, who):
         return out.at[
@@ -439,13 +454,11 @@
         done[h, j] = (mixed * scale).astype(BF16)
 
     for h in range(heads):
-        if h > 0:
-            wstep(2 + h, Z - 1)
+        got_query(2 + h, far)
         for b in range(nb):
             attend(h, 1 - y, b)
             give(h, b).start()
-        if h + 1 < heads:
-            begin_query(h + 1)
+    for h in range(heads):
         for b in range(nb):
             attend(h, y, b)
             keep(h, b).start()
@@ -462,22 +475,32 @@
                 to_y,
             ).wait_recv()
 
-    @pl.when(has_r)
-    def _():
-        state_copy.wait_send()
+    for to in range(1, Z):
+
+        @pl.when(to > z)
+        def _(to=to):
+            state_copy(to).wait_send()
 
     dec_copy.wait_send()
     for n in range(len(parts)):
         wpair(n).wait_send()
+    for n in range(2):
         for at in range(Z):
 
             @pl.when(has_r & (at <= z))
-            def _():
+            def _(at=at):
                 wright(n, at).wait_send()
 
             @pl.when(has_l & (at >= z))
-            def _():
+            def _(at=at):
                 wleft(n, at).wait_send()
+
+    for n in range(2, len(parts)):
+        for to in range(Z):
+
+            @pl.when(to != z)
+            def _(to=to):
+                wdirect(n, to).wait_send()
 
     for i in range(PIECES):
         own_tok(X, i, to_x).wait_send()
@@ -520,8 +543,10 @@
             pltpu.VMEM((heads, 2 * rows, HEAD), F32),
             pltpu.VMEM((heads, 2 * nb, HEAD, HEAD), F32),
             pltpu.VMEM((heads, 2 * nb, HEAD, HEAD), F32),
+            pltpu.VMEM((2, rows, half), F32),
             pltpu.VMEM((heads, HEAD, HEAD), F32),
-            pltpu.VMEM((heads, HEAD, HEAD), F32),
+            pltpu.VMEM((Z, heads, HEAD + 8, HEAD), F32),
+            pltpu.VMEM((heads, HEAD + 8, HEAD), F32),
             pltpu.VMEM((heads, 2 * nb, BLK, HEAD), BF16),
             dma((7, PIECES)),
             dma((7, PIECES)),
@@ -531,7 +556,9 @@
             dma((parts, Z)),
             dma((parts, Z)),
             dma((parts, Z)),
-            dma((6,)),
+            dma((4,)),
+            dma((Z,)),
+            dma((Z,)),
             dma((heads, nb)),
             dma((heads, nb)),
             dma((heads, nb)),

time: 156 us -> 135 us (0.87)
  Pallas kernels: 154 us -> 133 us
    pallas_call x1, Pallas kernels: 154 us -> 133 us  [on_device(): pl.pallas_call(functools.partial(kernel, S, Fn), out_shape=jax.ShapeDtype...]
where the time goes in v3:
time: 135 us
  Pallas kernels  133 us (99%)
  local copies, waits for them, and re-layouts  1.72 us (1%)
    pallas_call x1, Pallas kernels, on_device(): pl.pallas_call(functools.partial(kernel, S, Fn), out_shape=jax.ShapeDtype...  133 us

profile of v3, /device:TPU:24, one launch (start us, length us, event | category | flops | bytes accessed | tf_op | source)
XLA Modules:
  0.0 134.9 jit_solution(8292258543202017962)
XLA Ops:
  0.0 0.7 reshape.3
  0.8 133.2 %shard_map.37 = bf16[1024,512]{1,0:T(8,128)(2,1)S(1)} custom-call(bf16[1024,1024]{1,0:T(8,128)(2,1)} %tok_in.1, bf16[3,512,512]{2,1,0:T(8,128)(2,1)} %proj_in.1, f32[2,8,512]{2,1,0:T(8,128)S(1)} %pad.4.dec_in), custom_call_target="tpu_custom_call" | custom-call | tf_op jit(solution)/shard_map/pallas_call | solution.py:530
  134.0 1.0 copy.5
  (1 shorter events, 0.0 us)

commit v4 on v3

--- a/solution.py
+++ b/solution.py
@@ -145,9 +145,7 @@
         got_tok(D, i)
         tcopy(CD, i, to_c, place[D]).start()
 
-    parts = [(1, 0, half), (2, 0, half)]
-    for h in range(heads):
-        parts.append((0, h * HEAD, HEAD))
+    parts = [(1, 0, half), (2, 0, half), (0, 0, half)]
 
     def wslot(n, at):
         p, lo, width = parts[n]
@@ -244,7 +242,8 @@
         wlocal(n).start()
     for i in range(PIECES):
         own_tok(X, i, to_x).start()
-        own_tok(Y, i, to_y).start()
+        if not via_y(i):
+            own_tok(Y, i, to_y).start()
     for i in range(PIECES):
         own_tok(C, i, to_c).start()
     for n in range(2, len(parts)):
@@ -328,21 +327,21 @@
             for kind in kinds:
                 got_tok(kind, j)
 
-    def begin_query(h):
+    def begin_query():
         def tile(i, _):
             yy, b = i // nb, i % nb
             r = pl.ds(pl.multiple_of(b * BLK, BLK), BLK)
-            qacc[h, pl.ds(pl.multiple_of(i * BLK, BLK), BLK), :] = partial(2 + h, yy, r)
+            qacc[pl.ds(pl.multiple_of(i * BLK, BLK), BLK), :] = partial(2, yy, r)
             return 0
 
         lax.fori_loop(0, 2 * nb, tile, 0)
 
+    wsteps(0, 0)
+    wsteps(1, 0)
     side_step(0)
     pair_step(0)
-    wsteps(0, 0)
-    wsteps(1, 0)
-    for n in range(2, len(parts)):
-        wpair(n).start()
+    own_tok(Y, PIECES - 1, to_y).start()
+    wpair(2).start()
     for i in range(1, PIECES - 1):
         side_step(i)
         pair_step(i)
@@ -350,8 +349,7 @@
     wsteps(0, 1)
     wsteps(1, 1)
     pair_step(PIECES - 1)
-    for n in range(2, len(parts)):
-        own_query(n)
+    own_query(2)
     tok_local.wait()
     for i in range(nb):
         got_core((C, CX), i)
@@ -405,9 +403,8 @@
         def _(to=to):
             state_copy(to).start()
 
-    for h in range(heads):
-        got_near(2 + h)
-        begin_query(h)
+    got_near(2)
+    begin_query()
 
     enter[...] = jnp.zeros_like(enter)
     for at in range(Z - 1):
@@ -425,55 +422,47 @@
             before[h, j] = before[h, j] + jnp.exp(lead) * enter[h]
             lead = lead + block_end(h, j)
 
-    def place_out(h, b, who):
-        return out.at[
-            pl.ds(b * BLK, BLK), pl.ds(pl.multiple_of(who * half + h * HEAD, HEAD), HEAD)
-        ]
-
-    def give(h, b):
-        src = done.at[h, (1 - y) * nb + b]
-        return remote(src, place_out(h, b, y), osend.at[h, b], orecv.at[h, b], to_y)
-
-    def keep(h, b):
-        return pltpu.make_async_copy(done.at[h, y * nb + b], place_out(h, b, y), oloc.at[h, b])
-
-    def attend(h, yy, b):
-        at = h * nb + b
+    def place_out(b, who):
+        return out.at[pl.ds(b * BLK, BLK), pl.ds(pl.multiple_of(who * half, HEAD), half)]
+
+    def give(b):
+        src = done.at[(1 - y) * nb + b]
+        return remote(src, place_out(b, y), osend.at[b], orecv.at[b], to_y)
+
+    def keep(b):
+        return pltpu.make_async_copy(done.at[y * nb + b], place_out(b, y), oloc.at[b])
+
+    def attend(yy, b):
         j = yy * nb + b
-        hc = slice(h * HEAD, (h + 1) * HEAD)
         r = pl.ds(pl.multiple_of(j * BLK, BLK), BLK)
-        total = qacc[h, r, :] + chunk(2 + h, yy, pl.ds(b * BLK, BLK), far)
-        q, k, v = silu(total).astype(BF16), keys[r, hc], vals[r, hc]
-        scores = dot(q, k, ((1,), (1,)))
-        weights = (fade[h, j] * scores).astype(BF16)
-        high, low = split(before[h, j])
-        inter = dot(q, jnp.concatenate([high, low], axis=1))
-        inter = inter[:, :HEAD] + inter[:, HEAD:]
-        mixed = dot(weights, v) + jnp.exp(cols[yy, :, at : at + 1]) * inter
-        scale = lax.rsqrt(jnp.mean(mixed * mixed, axis=-1, keepdims=True) + 1e-6)
-        done[h, j] = (mixed * scale).astype(BF16)
-
-    for h in range(heads):
-        got_query(2 + h, far)
-        for b in range(nb):
-            attend(h, 1 - y, b)
-            give(h, b).start()
-    for h in range(heads):
-        for b in range(nb):
-            attend(h, y, b)
-            keep(h, b).start()
-
-    for h in range(heads):
-        for b in range(nb):
-            keep(h, b).wait()
-            give(h, b).wait_send()
-            remote(
-                done.at[h, y * nb + b],
-                place_out(h, b, 1 - y),
-                osend.at[h, b],
-                orecv.at[h, b],
-                to_y,
-            ).wait_recv()
+        queries = silu(qacc[r, :] + chunk(2, yy, pl.ds(b * BLK, BLK), far)).astype(BF16)
+        for h in range(heads):
+            at = h * nb + b
+            hc = slice(h * HEAD, (h + 1) * HEAD)
+            q, k, v = queries[:, hc], keys[r, hc], vals[r, hc]
+            scores = dot(q, k, ((1,), (1,)))
+            weights = (fade[h, j] * scores).astype(BF16)
+            high, low = split(before[h, j])
+            inter = dot(q, jnp.concatenate([high, low], axis=1))
+            inter = inter[:, :HEAD] + inter[:, HEAD:]
+            mixed = dot(weights, v) + jnp.exp(cols[yy, :, at : at + 1]) * inter
+            scale = lax.rsqrt(jnp.mean(mixed * mixed, axis=-1, keepdims=True) + 1e-6)
+            done[j, :, hc] = (mixed * scale).astype(BF16)
+
+    got_query(2, far)
+    for b in range(nb):
+        attend(1 - y, b)
+        give(b).start()
+    for b in range(nb):
+        attend(y, b)
+        keep(b).start()
+
+    for b in range(nb):
+        keep(b).wait()
+        give(b).wait_send()
+        remote(
+            done.at[y * nb + b], place_out(b, 1 - y), osend.at[b], orecv.at[b], to_y
+        ).wait_recv()
 
     for to in range(1, Z):
 
@@ -522,7 +511,7 @@
     half = width // 2
     heads = half // HEAD
     nb = rows // BLK
-    parts = 2 + heads
+    parts = 3
     dec = log_decay.T.reshape(2, heads * nb, BLK)
     dec = jnp.pad(dec, ((0, 0), (0, 8 - heads * nb), (0, 0)))
     dma = pltpu.SemaphoreType.DMA
@@ -540,14 +529,14 @@
             pltpu.VMEM((heads, 2 * nb, BLK, BLK), F32),
             pltpu.VMEM((2 * rows, half), BF16),
             pltpu.VMEM((2 * rows, half), BF16),
-            pltpu.VMEM((heads, 2 * rows, HEAD), F32),
+            pltpu.VMEM((2 * rows, half), F32),
             pltpu.VMEM((heads, 2 * nb, HEAD, HEAD), F32),
             pltpu.VMEM((heads, 2 * nb, HEAD, HEAD), F32),
             pltpu.VMEM((2, rows, half), F32),
             pltpu.VMEM((heads, HEAD, HEAD), F32),
             pltpu.VMEM((Z, heads, HEAD + 8, HEAD), F32),
             pltpu.VMEM((heads, HEAD + 8, HEAD), F32),
-            pltpu.VMEM((heads, 2 * nb, BLK, HEAD), BF16),
+            pltpu.VMEM((2 * nb, BLK, half), BF16),
             dma((7, PIECES)),
             dma((7, PIECES)),
             dma((parts,)),
@@ -559,9 +548,9 @@
             dma((4,)),
             dma((Z,)),
             dma((Z,)),
-            dma((heads, nb)),
-            dma((heads, nb)),
-            dma((heads, nb)),
+            dma((nb,)),
+            dma((nb,)),
+            dma((nb,)),
         ],
         compiler_params=pltpu.CompilerParams(
             collective_id=0, has_side_effects=True, vmem_limit_bytes=52 * 1024 * 1024

time: 135 us -> 140 us (1.037)
  Pallas kernels: 133 us -> 138 us
    pallas_call x1, Pallas kernels: 133 us -> 138 us  [on_device(): pl.pallas_call(functools.partial(kernel, S, Fn), out_shape=jax.ShapeDtype...]
where the time goes in v4:
time: 140 us
  Pallas kernels  138 us (99%)
  local copies, waits for them, and re-layouts  1.72 us (1%)
    pallas_call x1, Pallas kernels, on_device(): pl.pallas_call(functools.partial(kernel, S, Fn), out_shape=jax.ShapeDtype...  138 us

profile of v4, /device:TPU:24, one launch (start us, length us, event | category | flops | bytes accessed | tf_op | source)
XLA Modules:
  0.0 139.7 jit_solution(17640468077395756245)
XLA Ops:
  0.0 0.7 reshape.3
  0.8 138.0 %shard_map.37 = bf16[1024,512]{1,0:T(8,128)(2,1)S(1)} custom-call(bf16[1024,1024]{1,0:T(8,128)(2,1)} %tok_in.1, bf16[3,512,512]{2,1,0:T(8,128)(2,1)} %proj_in.1, f32[2,8,512]{2,1,0:T(8,128)S(1)} %pad.4.dec_in), custom_call_target="tpu_custom_call" | custom-call | tf_op jit(solution)/shard_map/pallas_call | solution.py:519
  138.7 1.0 copy.5
  (1 shorter events, 0.0 us)

commit v5 on v4

--- a/solution.py
+++ b/solution.py
@@ -147,9 +147,9 @@
 
     parts = [(1, 0, half), (2, 0, half), (0, 0, half)]
 
-    def wslot(n, at):
+    def wslot(n, at, yy):
         p, lo, width = parts[n]
-        return wts.at[p, at, :, :, pl.ds(lo, width)]
+        return wts.at[p, at, yy, :, pl.ds(lo, width)]
 
     def wmember(n, yy):
         p, lo, width = parts[n]
@@ -165,55 +165,58 @@
     def wpair(n):
         return remote(wsource(n, 1 - y), wmember(n, y), wysend.at[n], wyrecv.at[n], to_y)
 
-    def wright(n, at):
-        slot = wslot(n, at)
-        return remote(slot, slot, wrsend.at[n, at], wrecv.at[n, at], to_r)
-
-    def wleft(n, at):
-        slot = wslot(n, at)
-        return remote(slot, slot, wlsend.at[n, at], wrecv.at[n, at], to_l)
-
-    def own_part(n):
-        wlocal(n).wait()
+    def wright(n, at, yy):
+        slot = wslot(n, at, yy)
+        return remote(slot, slot, wrsend.at[n, at, yy], wrecv.at[n, at, yy], to_r)
+
+    def wleft(n, at, yy):
+        slot = wslot(n, at, yy)
+        return remote(slot, slot, wlsend.at[n, at, yy], wrecv.at[n, at, yy], to_l)
+
+    def got_pair(n):
         remote(wsource(n, y), wmember(n, 1 - y), wysend.at[n], wyrecv.at[n], to_y).wait_recv()
 
+    def own_part(n, yy):
         @pl.when(has_r)
         def _():
-            wright(n, z).start()
+            wright(n, z, yy).start()
 
         @pl.when(has_l)
         def _():
-            wleft(n, z).start()
+            wleft(n, z, yy).start()
 
     def wstep(n, d):
-        @pl.when(z - d >= 0)
-        def _():
-            wright(n, z - d).wait_recv()
-
-            @pl.when(has_r)
-            def _():
-                wright(n, z - d).start()
-
-        @pl.when(z + d <= Z - 1)
-        def _():
-            wleft(n, z + d).wait_recv()
-
-            @pl.when(has_l)
-            def _():
-                wleft(n, z + d).start()
-
-    def wdirect(n, to):
-        slot = wslot(n, z)
-        return remote(slot, slot, wrsend.at[n, to], wrecv.at[n, z], (to * 2 + y, f))
+        for yy in (y, 1 - y):
+
+            @pl.when(z - d >= 0)
+            def _(yy=yy):
+                wright(n, z - d, yy).wait_recv()
+
+                @pl.when(has_r)
+                def _():
+                    wright(n, z - d, yy).start()
+
+            @pl.when(z + d <= Z - 1)
+            def _(yy=yy):
+                wleft(n, z + d, yy).wait_recv()
+
+                @pl.when(has_l)
+                def _():
+                    wleft(n, z + d, yy).start()
+
+    def wdirect(n, to, yy):
+        slot = wslot(n, z, yy)
+        return remote(slot, slot, wrsend.at[n, to, yy], wrecv.at[n, z, yy], (to * 2 + y, f))
 
     def own_query(n):
         wlocal(n).wait()
-        remote(wsource(n, y), wmember(n, 1 - y), wysend.at[n], wyrecv.at[n], to_y).wait_recv()
+        got_pair(n)
         for to in range(Z):
 
             @pl.when(to != z)
             def _(to=to):
-                wdirect(n, to).start()
+                for yy in range(2):
+                    wdirect(n, to, yy).start()
 
     near = (z // (Z - 1)) * (Z - 1)
     far = Z - 1 - near
@@ -221,7 +224,8 @@
     def got_query(n, at):
         @pl.when(at != z)
         def _():
-            wright(n, at).wait_recv()
+            for yy in range(2):
+                wright(n, at, yy).wait_recv()
 
     def got_near(n):
         got_query(n, near)
@@ -238,20 +242,23 @@
     dec_local = pltpu.make_async_copy(dec_in.at[y], dec.at[y], misc.at[2])
     for n in (0, 1):
         wpair(n).start()
-    for n in range(2):
         wlocal(n).start()
     for i in range(PIECES):
         own_tok(X, i, to_x).start()
+    for n in (0, 1):
+        wlocal(n).wait()
+        own_part(n, y)
+    for i in range(PIECES):
+        own_tok(C, i, to_c).start()
+    wlocal(2).start()
+    tok_local = pltpu.make_async_copy(tok_in, tok.at[mine], misc.at[3])
+    tok_local.start()
+    for n in (0, 1):
+        got_pair(n)
+        own_part(n, 1 - y)
+    for i in range(PIECES):
         if not via_y(i):
             own_tok(Y, i, to_y).start()
-    for i in range(PIECES):
-        own_tok(C, i, to_c).start()
-    for n in range(2, len(parts)):
-        wlocal(n).start()
-    tok_local = pltpu.make_async_copy(tok_in, tok.at[mine], misc.at[3])
-    tok_local.start()
-    own_part(0)
-    own_part(1)
 
     dec_local.start()
     dec_local.wait()
@@ -473,23 +480,22 @@
     dec_copy.wait_send()
     for n in range(len(parts)):
         wpair(n).wait_send()
-    for n in range(2):
-        for at in range(Z):
-
-            @pl.when(has_r & (at <= z))
-            def _(at=at):
-                wright(n, at).wait_send()
-
-            @pl.when(has_l & (at >= z))
-            def _(at=at):
-                wleft(n, at).wait_send()
-
-    for n in range(2, len(parts)):
-        for to in range(Z):
-
-            @pl.when(to != z)
-            def _(to=to):
-                wdirect(n, to).wait_send()
+    for at in range(Z):
+        for n in range(2):
+            for yy in range(2):
+
+                @pl.when(has_r & (at <= z))
+                def _(n=n, at=at, yy=yy):
+                    wright(n, at, yy).wait_send()
+
+                @pl.when(has_l & (at >= z))
+                def _(n=n, at=at, yy=yy):
+                    wleft(n, at, yy).wait_send()
+
+        @pl.when(at != z)
+        def _(at=at):
+            for yy in range(2):
+                wdirect(2, at, yy).wait_send()
 
     for i in range(PIECES):
         own_tok(X, i, to_x).wait_send()
@@ -542,9 +548,9 @@
             dma((parts,)),
             dma((parts,)),
             dma((parts,)),
-            dma((parts, Z)),
-            dma((parts, Z)),
-            dma((parts, Z)),
+            dma((parts, Z, 2)),
+            dma((parts, Z, 2)),
+            dma((parts, Z, 2)),
             dma((4,)),
             dma((Z,)),
             dma((Z,)),

time: 140 us -> 139 us (level)
  no operation moved by 1% of the time
where the time goes in v5:
time: 139 us; the launch traced here: 138 us
  Pallas kernels  137 us (99%)
  local copies, waits for them, and re-layouts  1.72 us (1%)
    pallas_call x1, Pallas kernels, on_device(): pl.pallas_call(functools.partial(kernel, S, Fn), out_shape=jax.ShapeDtype...  137 us

profile of v5, /device:TPU:24, one launch (start us, length us, event | category | flops | bytes accessed | tf_op | source)
XLA Modules:
  0.0 138.4 jit_solution(15659926362694880826)
XLA Ops:
  0.0 0.7 reshape.3
  0.8 136.7 %shard_map.37 = bf16[1024,512]{1,0:T(8,128)(2,1)S(1)} custom-call(bf16[1024,1024]{1,0:T(8,128)(2,1)} %tok_in.1, bf16[3,512,512]{2,1,0:T(8,128)(2,1)} %proj_in.1, f32[2,8,512]{2,1,0:T(8,128)S(1)} %pad.4.dec_in), custom_call_target="tpu_custom_call" | custom-call | tf_op jit(solution)/shard_map/pallas_call | solution.py:525
  137.4 1.0 copy.5
  (1 shorter events, 0.0 us)

commit v6 on v5

--- a/solution.py
+++ b/solution.py
@@ -44,6 +44,7 @@
     keys,
     vals,
     qacc,
+    qry,
     fresh,
     before,
     kvacc,
@@ -402,8 +403,9 @@
             before[h, j] = state
             state = jnp.exp(block_end(h, j)) * state + fresh[h, j]
             lead = lead + block_end(h, j)
-        s_out[h, 0:HEAD, :] = state
-        s_out[h, HEAD : HEAD + 8, :] = jnp.broadcast_to(lead, (8, HEAD))
+        s_out[h, 0:HEAD, :] = state.astype(BF16)
+        high, low = split(jnp.broadcast_to(jnp.exp(lead), (8, HEAD)))
+        s_out[h, HEAD : HEAD + 16, :] = jnp.concatenate([high, low], axis=0)
     for to in range(1, Z):
 
         @pl.when(to > z)
@@ -413,22 +415,6 @@
     got_near(2)
     begin_query()
 
-    enter[...] = jnp.zeros_like(enter)
-    for at in range(Z - 1):
-
-        @pl.when(at < z)
-        def _(at=at):
-            remote(s_out, s_in.at[at], ssend.at[at], srecv.at[at], (at * 2 + y, f)).wait_recv()
-            for h in range(heads):
-                decay = jnp.exp(s_in[at, h, HEAD : HEAD + 1, :])
-                enter[h] = decay * enter[h] + s_in[at, h, 0:HEAD, :]
-
-    for h in range(heads):
-        lead = jnp.zeros((1, 1), F32)
-        for j in range(2 * nb):
-            before[h, j] = before[h, j] + jnp.exp(lead) * enter[h]
-            lead = lead + block_end(h, j)
-
     def place_out(b, who):
         return out.at[pl.ds(b * BLK, BLK), pl.ds(pl.multiple_of(who * half, HEAD), half)]
 
@@ -438,30 +424,63 @@
 
     def keep(b):
         return pltpu.make_async_copy(done.at[y * nb + b], place_out(b, y), oloc.at[b])
+
+    def from_state(q, h, j, run):
+        high, low = split(before[h, j])
+        inter = dot(q, jnp.concatenate([high, low], axis=1))
+        return jnp.exp(run) * (inter[:, :HEAD] + inter[:, HEAD:])
 
     def attend(yy, b):
         j = yy * nb + b
         r = pl.ds(pl.multiple_of(j * BLK, BLK), BLK)
         queries = silu(qacc[r, :] + chunk(2, yy, pl.ds(b * BLK, BLK), far)).astype(BF16)
+        qry[r, :] = queries
         for h in range(heads):
             at = h * nb + b
             hc = slice(h * HEAD, (h + 1) * HEAD)
             q, k, v = queries[:, hc], keys[r, hc], vals[r, hc]
             scores = dot(q, k, ((1,), (1,)))
             weights = (fade[h, j] * scores).astype(BF16)
-            high, low = split(before[h, j])
-            inter = dot(q, jnp.concatenate([high, low], axis=1))
-            inter = inter[:, :HEAD] + inter[:, HEAD:]
-            mixed = dot(weights, v) + jnp.exp(cols[yy, :, at : at + 1]) * inter
+            qacc[r, hc] = dot(weights, v) + from_state(q, h, j, cols[yy, :, at : at + 1])
+
+    def complete(yy, b):
+        j = yy * nb + b
+        r = pl.ds(pl.multiple_of(j * BLK, BLK), BLK)
+        for h in range(heads):
+            at = h * nb + b
+            hc = slice(h * HEAD, (h + 1) * HEAD)
+            mixed = qacc[r, hc] + from_state(qry[r, hc], h, j, cols[yy, :, at : at + 1])
             scale = lax.rsqrt(jnp.mean(mixed * mixed, axis=-1, keepdims=True) + 1e-6)
             done[j, :, hc] = (mixed * scale).astype(BF16)
 
     got_query(2, far)
     for b in range(nb):
         attend(1 - y, b)
+    for b in range(nb):
+        attend(y, b)
+
+    enter[...] = jnp.zeros_like(enter)
+    for at in range(Z - 1):
+
+        @pl.when(at < z)
+        def _(at=at):
+            remote(s_out, s_in.at[at], ssend.at[at], srecv.at[at], (at * 2 + y, f)).wait_recv()
+            for h in range(heads):
+                terms = s_in[at, h, HEAD : HEAD + 16, :].astype(F32)
+                decay = terms[0:1] + terms[8:9]
+                enter[h] = decay * enter[h] + s_in[at, h, 0:HEAD, :].astype(F32)
+
+    for h in range(heads):
+        lead = jnp.zeros((1, 1), F32)
+        for j in range(2 * nb):
+            before[h, j] = jnp.exp(lead) * enter[h]
+            lead = lead + block_end(h, j)
+
+    for b in range(nb):
+        complete(1 - y, b)
         give(b).start()
     for b in range(nb):
-        attend(y, b)
+        complete(y, b)
         keep(b).start()
 
     for b in range(nb):
@@ -536,12 +555,13 @@
             pltpu.VMEM((2 * rows, half), BF16),
             pltpu.VMEM((2 * rows, half), BF16),
             pltpu.VMEM((2 * rows, half), F32),
+            pltpu.VMEM((2 * rows, half), BF16),
             pltpu.VMEM((heads, 2 * nb, HEAD, HEAD), F32),
             pltpu.VMEM((heads, 2 * nb, HEAD, HEAD), F32),
             pltpu.VMEM((2, rows, half), F32),
             pltpu.VMEM((heads, HEAD, HEAD), F32),
-            pltpu.VMEM((Z, heads, HEAD + 8, HEAD), F32),
-            pltpu.VMEM((heads, HEAD + 8, HEAD), F32),
+            pltpu.VMEM((Z, heads, HEAD + 16, HEAD), BF16),
+            pltpu.VMEM((heads, HEAD + 16, HEAD), BF16),
             pltpu.VMEM((2 * nb, BLK, half), BF16),
             dma((7, PIECES)),
             dma((7, PIECES)),

time: 139 us -> 139 us (level)
  no operation moved by 1% of the time
where the time goes in v6:
time: 139 us; the launch traced here: 138 us
  Pallas kernels  137 us (99%)
  local copies, waits for them, and re-layouts  1.72 us (1%)
    pallas_call x1, Pallas kernels, on_device(): pl.pallas_call(functools.partial(kernel, S, Fn), out_shape=jax.ShapeDtype...  137 us

profile of v6, /device:TPU:24, one launch (start us, length us, event | category | flops | bytes accessed | tf_op | source)
XLA Modules:
  0.0 138.4 jit_solution(15975098750320838561)
XLA Ops:
  0.0 0.7 reshape.3
  0.8 136.7 %shard_map.37 = bf16[1024,512]{1,0:T(8,128)(2,1)S(1)} custom-call(bf16[1024,1024]{1,0:T(8,128)(2,1)} %tok_in.1, bf16[3,512,512]{2,1,0:T(8,128)(2,1)} %proj_in.1, f32[2,8,512]{2,1,0:T(8,128)S(1)} %pad.4.dec_in), custom_call_target="tpu_custom_call" | custom-call | tf_op jit(solution)/shard_map/pallas_call | solution.py:544
  137.4 1.0 copy.5
  (1 shorter events, 0.0 us)
